TPU v7x, 32 devices: a whole 2x2x4 slice. The times are simulated.
32 devices in a mesh: group: 2 (over x), src: 8 (over z, y), tile: 2 (over core).
Axes of the slice: x: 2, y: 2, z: 4, core: 2. Of those that a mesh axis runs over, the one named last changes fastest.
Arguments:
- near_field: bfloat16 [4, 64, 2, 3, 512], P(('group', 'tile'), 'src'), parts along dimension 0, may hold values from -6 to 6
- x_taps: bfloat16 [8, 2, 8, 65], P('src'), may hold values from -0.5 to 0.5
- y_taps: bfloat16 [8, 2, 8, 65], P('src'), may hold values from -0.1875 to 0.1875
- source_weight: float32 [8], P('src'), may hold values from 0.0125 to 0.125
Outputs:
- intensity: float32 [4, 64, 512], P(('group', 'tile'), 'src'), parts along dimension 0
There are 2 independent parts, one for each index of `group`. A program takes and returns all parts, laid end to end along the dimension named above; an argument that names none is the same for every part. Nothing has to cross between parts.
All inputs are finite; a program needn't handle non-finite values.
Results may differ from a plain program's by a relative error of at most 0.00054.
Values may be sent and summed in bfloat16 or wider, within the bound.
No kernel may reach another device: no remote copies, remote signals or barrier semaphores. Data moves between devices by JAX's collectives and lax.ppermute only.
A program may use at most 128 MiB of HBM per device.

v0:
```python
import functools

import jax
import jax.numpy as jnp
from jax import lax
from jax.experimental import pallas as pl
from jax.experimental.pallas import tpu as pltpu
from jax.sharding import PartitionSpec as P

LANES = 128
F32 = jnp.float32
BF16 = jnp.bfloat16


def send_kernel(
    rim, field_hbm, x_taps_hbm, y_taps_hbm, weight_ref, send_ref, field_ref, x_taps_ref, y_taps_ref, sems
):
    pairs = ((field_hbm, field_ref), (x_taps_hbm, x_taps_ref), (y_taps_hbm, y_taps_ref))
    copies = [pltpu.make_async_copy(source, target, sems.at[n]) for n, (source, target) in enumerate(pairs)]
    for copy in copies:
        copy.start()
    for copy in copies:
        copy.wait()
    _, rows, comps, _, width = field_ref.shape
    sources, tiles, height, lanes = send_ref.shape
    ranks, taps = x_taps_ref.shape[2:]
    mine = width // (sources * tiles)
    window = mine + 2 * rim
    edge = jnp.zeros((rows, rim), F32)
    field = field_ref[0].astype(F32)
    padded = [
        [jnp.concatenate([edge, field[:, comp, part, :], edge], axis=1) for part in range(2)] for comp in range(comps)
    ]
    lower = lax.axis_index("tile") == 0
    lines = [
        jnp.where(lower, x_taps_ref[0, part].astype(F32), y_taps_ref[0, part].astype(F32)) for part in range(2)
    ]
    weight = jnp.full((ranks, 1), weight_ref[0], F32)
    high = weight.astype(BF16).astype(F32)
    middle = (weight - high).astype(BF16).astype(F32)
    low = weight - high - middle
    last = [line[:, taps - 1 :] for line in lines] + [high, middle, low]
    last.append(jnp.zeros((ranks, taps - 1 - len(last)), F32))
    spare = jnp.concatenate([line[:, : taps - 1] for line in lines] + [jnp.concatenate(last, axis=1)], axis=0)
    spares = [spare[:, :rim], spare[:, rim:]]
    if window < LANES - rim:
        gap = jnp.zeros((height, LANES - rim - window), F32)
        spares = [jnp.concatenate([gap, part], axis=1) for part in spares]
    for device in range(sources * tiles):
        at = device * mine
        cells = []
        for part in range(2):
            plane = [padded[comp][part][:, at : at + window] for comp in range(comps)]
            cells += [jnp.concatenate(plane, axis=0), spares[part]]
        source, tile = divmod(device, tiles)
        send_ref[source, tile] = jnp.concatenate(cells, axis=1).astype(BF16)


def rolled(line, count):
    return pltpu.roll(jnp.broadcast_to(line, (count, line.shape[1])), 0, 1, stride=1, stride_axis=0)


def image_kernel(rim, comps, rows, ranks, got_ref, out_ref, field_ref, taps_ref, column_ref, lhs_ref, row_ref, total_ref):
    sources, tiles, _, lanes = got_ref.shape
    mine, slab_rows = total_ref.shape
    window = mine + 2 * rim
    tile_rows = sources * rows
    chunks = slab_rows // LANES
    windows = row_ref.shape[1]
    half_lanes = LANES // 2
    for tile in range(tiles):
        cells = got_ref[:, tile].astype(F32)
        for comp in range(comps):
            some = cells[:, comp * rows : (comp + 1) * rows, :].reshape(tile_rows, lanes).astype(BF16)
            at = comp * slab_rows + tile * tile_rows
            field_ref[at : at + tile_rows, :] = some

    tap = lax.broadcasted_iota(jnp.int32, (2 * rim, LANES), 0)
    lane = lax.broadcasted_iota(jnp.int32, (2 * rim, LANES), 1)
    x_place = (lane == tap).astype(BF16)
    y_place = (lane == (rim - tap) % LANES).astype(BF16)
    x_last = (lane[:1] == 2 * rim).astype(F32)
    y_last = (lane[:1] == LANES - rim).astype(F32)
    for n, (place, last_place) in enumerate(((x_place, x_last), (y_place, y_last))):
        block = got_ref[:, n].astype(F32)
        taps = jnp.concatenate([block[:, :, LANES - rim : LANES], block[:, :, 2 * LANES - rim :]], axis=2)
        for part in range(2):
            first = taps[:, part * ranks : (part + 1) * ranks].reshape(sources * ranks, 2 * rim)
            last = taps[:, 2 * ranks : 3 * ranks].reshape(sources * ranks, 2 * rim)[:, part : part + 1]
            line = jnp.dot(first.astype(BF16), place, preferred_element_type=F32) + last * last_place
            taps_ref[2 * n + part] = line
    k = lax.broadcasted_iota(jnp.int32, (LANES, LANES), 0)
    i = lax.broadcasted_iota(jnp.int32, (LANES, LANES), 1)
    near = jnp.abs(i - k) < half_lanes
    masks = [near] if windows == 1 else [k - i > half_lanes, near, k - i < -half_lanes]
    total_ref[...] = jnp.zeros_like(total_ref)

    def bands(source, slot):
        at = source * ranks if isinstance(source, int) else pl.multiple_of(source * ranks, ranks)
        lines = [taps_ref[n, pl.ds(at, ranks), :] for n in range(4)]
        y_lines = lines[2:]
        for r in range(ranks):
            re, im = (rolled(line[r : r + 1], mine) for line in lines[:2])
            top = 2 * r * mine
            column_ref[slot, top : top + mine, :LANES] = re.astype(column_ref.dtype)
            column_ref[slot, top : top + mine, LANES:] = (-im).astype(column_ref.dtype)
            column_ref[slot, top + mine : top + 2 * mine, :LANES] = im.astype(column_ref.dtype)
            column_ref[slot, top + mine : top + 2 * mine, LANES:] = re.astype(column_ref.dtype)
        for r in range(ranks):
            for part in range(2):
                ring = rolled(y_lines[part][r : r + 1], LANES)
                for n, mask in enumerate(masks):
                    row_ref[slot, n, r * LANES : (r + 1) * LANES, part * LANES : (part + 1) * LANES] = jnp.where(
                        mask, ring, 0.0
                    ).astype(BF16)

    def column_pass(slot):
        passed = lax.dot_general(
            column_ref[slot].astype(BF16), field_ref[...], (((1,), (1,)), ((), ())), preferred_element_type=F32
        )
        for chunk in range(chunks):
            for r in range(ranks):
                cells = []
                for part in range(2):
                    for comp in range(comps):
                        top, left = (2 * r + part) * mine, comp * slab_rows + chunk * LANES
                        cells.append(passed[top : top + mine, left : left + LANES])
                lhs_ref[slot, chunk, :, r * LANES : (r + 1) * LANES] = jnp.concatenate(cells, axis=0).astype(BF16)

    def row_pass(source, slot):
        weight = got_ref[source, 0].astype(F32)[2 * ranks : 2 * ranks + 1, LANES - rim : LANES]
        weight = weight[:, 2:3] + weight[:, 3:4] + weight[:, 4:5]
        for chunk in range(chunks):
            image = None
            for n in range(windows):
                other = chunk + n - windows // 2
                if 0 <= other < chunks:
                    term = jnp.dot(lhs_ref[slot, other], row_ref[slot, n], preferred_element_type=F32)
                    image = term if image is None else image + term
            of_re, of_im = image[: comps * mine], image[comps * mine :]
            image_re = of_re[:, :LANES] - of_im[:, LANES:]
            image_im = of_re[:, LANES:] + of_im[:, :LANES]
            square = image_re * image_re + image_im * image_im
            power = square[:mine]
            for comp in range(1, comps):
                power = power + square[comp * mine : (comp + 1) * mine]
            total_ref[:, chunk * LANES : (chunk + 1) * LANES] += weight * power

    if sources <= 8:
        bands(0, 0)
        column_pass(0)
        bands(1, 1)
        for source in range(sources):
            if source + 1 < sources:
                column_pass(source + 1)
            row_pass(source, source)
            if source + 2 < sources:
                bands(source + 2, source + 2)
    else:

        def one_source(source, _):
            bands(source, 0)
            column_pass(0)
            row_pass(source, 0)

        lax.fori_loop(0, sources, one_source, None)
    for chunk in range(chunks):
        lines = total_ref[:, chunk * LANES : (chunk + 1) * LANES].T
        for piece in range(LANES // rows):
            tile, source = divmod((chunk * LANES) // rows + piece, sources)
            block = lines[piece * rows : (piece + 1) * rows]
            step = out_ref.shape[2]
            groups = [block[n : n + step] for n in range(0, rows, step)]
            out_ref[source, tile] = jnp.concatenate(groups, axis=1)


def merge_kernel(parts_ref, out_ref):
    devices = parts_ref.shape[0]
    mine = out_ref.shape[2] // devices
    blocks = []
    for device in range(devices):
        part = parts_ref[device]
        groups = [part[:, at : at + mine] for at in range(0, part.shape[1], mine)]
        blocks.append(jnp.concatenate(groups, axis=0))
    out_ref[0] = jnp.concatenate(blocks, axis=1)


def per_device(near_field, x_taps, y_taps, source_weight):
    sources, tiles = lax.axis_size("src"), lax.axis_size("tile")
    _, rows, _, comps, width = near_field.shape
    ranks, taps = x_taps.shape[-2:]
    rim = (taps - 1) // 2
    devices = sources * tiles
    mine = width // devices
    lanes = 2 * LANES
    slab_rows = devices * rows
    chunks = slab_rows // LANES
    windows = 1 if chunks == 1 else 3
    height = comps * rows
    step = max(1, rows * mine // LANES)
    params = pltpu.CompilerParams(vmem_limit_bytes=48 * 1024 * 1024)
    whole = pl.BlockSpec(memory_space=pltpu.VMEM)

    def in_hbm(array):
        return pltpu.with_memory_space_constraint(array, pltpu.HBM)

    send = pl.pallas_call(
        functools.partial(send_kernel, rim),
        out_shape=jax.ShapeDtypeStruct((sources, tiles, height, lanes), BF16),
        in_specs=[pl.BlockSpec(memory_space=pltpu.HBM)] * 3 + [pl.BlockSpec(memory_space=pltpu.SMEM)],
        out_specs=whole,
        scratch_shapes=[
            pltpu.VMEM((1, rows, comps, 2, width), BF16),
            pltpu.VMEM(x_taps.shape, BF16),
            pltpu.VMEM(y_taps.shape, BF16),
            pltpu.SemaphoreType.DMA((3,)),
        ],
        compiler_params=params,
        name="send_columns",
    )(in_hbm(near_field.transpose(0, 1, 3, 2, 4)), in_hbm(x_taps), in_hbm(y_taps), source_weight)
    got = lax.all_to_all(send.reshape(devices, height, lanes), ("src", "tile"), 0, 0).reshape(send.shape)
    slots = sources if sources <= 8 else 1
    image = pl.pallas_call(
        functools.partial(image_kernel, rim, comps, rows, ranks),
        out_shape=jax.ShapeDtypeStruct((sources, tiles, step, rows // step * mine), F32),
        in_specs=[whole],
        out_specs=whole,
        scratch_shapes=[
            pltpu.VMEM((comps * slab_rows, lanes), BF16),
            pltpu.VMEM((4, sources * ranks, LANES), F32),
            pltpu.VMEM((slots, 2 * ranks * mine, lanes), BF16 if mine % 16 == 0 else F32),
            pltpu.VMEM((slots, chunks, 2 * comps * mine, ranks * LANES), BF16),
            pltpu.VMEM((slots, windows, ranks * LANES, 2 * LANES), BF16),
            pltpu.VMEM((mine, slab_rows), F32),
        ],
        compiler_params=params,
        name="image",
    )(got)
    parts = lax.all_to_all(image.reshape((devices,) + image.shape[2:]), ("src", "tile"), 0, 0)
    return pl.pallas_call(
        merge_kernel,
        out_shape=jax.ShapeDtypeStruct((1, rows, width), F32),
        in_specs=[whole],
        out_specs=whole,
        compiler_params=params,
        name="merge_columns",
    )(parts)


def solution(mesh):
    placed = (
        P(("group", "tile"), "src", None, None, None),
        P("src", None, None, None),
        P("src", None, None, None),
        P("src"),
    )
    return jax.shard_map(
        per_device,
        mesh=mesh,
        in_specs=placed,
        out_specs=P(("group", "tile"), "src", None),
        check_vma=False,
    )
```

profile of v0, /device:TPU:0, one launch (start us, length us, event | category | flops | bytes accessed | tf_op | source)
XLA Modules:
  0.0 30.6 jit_solution(4388554683601974872)
XLA Ops:
  0.7 1.1 %send_columns.1 = bf16[8,2,24,256]{3,2,1,0:T(8,128)(2,1)S(1)} custom-call(bf16[1,8,3,2,512]{4,3,2,1,0:T(2,128)(2,1)} %bitcast.7, bf16[1,2,8,65]{3,2,1,0:T(8,128)(2,1)} %x_taps_hbm.1, bf16[1,2,8,65]{3,2,1,0:T(8,128)(2,1)} %y_taps_hbm.1, f32[1]{0:T(128)S(6)} %copy.5.weight_ref), custom_call_target="tpu_custom_call" | custom-call | tf_op jit(solution)/shard_map/send_columns/pallas_call | solution.py:207
  1.7 16.2 %all_to_all.10 = bf16[16,24,256]{2,1,0:T(8,128)(2,1)S(1)} all-to-all(bf16[16,24,256]{2,1,0:T(8,128)(2,1)S(1)} %bitcast.5), channel_id=1, replica_groups=mesh['group'=2,'src'=8,'tile'=2] {'src','tile'}, dimensions={0} | all-to-all | bytes 393216 | tf_op jit(solution)/shard_map/all_to_all | solution.py:221
  17.9 2.8 %image.1 = f32[8,2,2,128]{3,2,1,0:T(2,128)S(1)} custom-call(bf16[8,2,24,256]{3,2,1,0:T(8,128)(2,1)S(1)} %bitcast.4), custom_call_target="tpu_custom_call" | custom-call | tf_op jit(solution)/shard_map/image/pallas_call | solution.py:223
  20.7 9.1 %all_to_all.11.parts_ref = f32[16,2,128]{2,1,0:T(2,128)S(1)} all-to-all(f32[16,2,128]{2,1,0:T(2,128)S(1)} %bitcast.6), channel_id=1, replica_groups=mesh['group'=2,'src'=8,'tile'=2] {'src','tile'}, dimensions={0} | all-to-all | bytes 32768 | tf_op jit(solution)/shard_map/all_to_all | solution.py:239
  29.8 0.8 %merge_columns.1 = f32[1,8,512]{2,1,0:T(8,128)} custom-call(f32[16,2,128]{2,1,0:T(2,128)S(1)} %all_to_all.11.parts_ref), custom_call_target="tpu_custom_call" | custom-call | tf_op jit(solution)/shard_map/merge_columns/pallas_call | solution.py:240
where the time goes:
time: 30.8 us; the launch traced here: 30.6 us
  blocking collectives  25.2 us (82%)
  Pallas kernels  4.64 us (15%)
  between operations  0.67 us (2%)
    all_to_all x1, blocking collectives, per_device(): lax.all_to_all(send.reshape(devices, height, lanes), ('src', 'tile'), 0, 0)  16.2 us
    all_to_all x1, blocking collectives, per_device(): lax.all_to_all(image.reshape((devices,) + image.shape[2:]), ('src', 'tile...  9.07 us
    pallas_call x1, Pallas kernels, per_device(): pl.pallas_call(functools.partial(image_kernel, rim, comps, rows, ranks),...  2.81 us
    pallas_call x1, Pallas kernels, per_device(): pl.pallas_call(functools.partial(send_kernel, rim), out_shape=jax.ShapeDt...  1.05 us
    pallas_call x1, Pallas kernels, per_device(): pl.pallas_call(merge_kernel, out_shape=jax.ShapeDtypeStruct((1, rows, wid...  0.78 us

commit v1 on v0

--- a/solution.py
+++ b/solution.py
@@ -110,8 +110,13 @@
             for part in range(2):
                 ring = rolled(y_lines[part][r : r + 1], LANES)
                 for n, mask in enumerate(masks):
-                    row_ref[slot, n, r * LANES : (r + 1) * LANES, part * LANES : (part + 1) * LANES] = jnp.where(
-                        mask, ring, 0.0
+                    band = [
+                        jnp.where(mask[:rim], ring[:rim], 0.0),
+                        ring[rim : LANES - rim] if n == windows // 2 else jnp.zeros((LANES - 2 * rim, LANES), F32),
+                        jnp.where(mask[LANES - rim :], ring[LANES - rim :], 0.0),
+                    ]
+                    row_ref[slot, n, r * LANES : (r + 1) * LANES, part * LANES : (part + 1) * LANES] = jnp.concatenate(
+                        band, axis=0
                     ).astype(BF16)
 
     def column_pass(slot):
@@ -153,9 +158,9 @@
         for source in range(sources):
             if source + 1 < sources:
                 column_pass(source + 1)
-            row_pass(source, source)
             if source + 2 < sources:
                 bands(source + 2, source + 2)
+            row_pass(source, source)
     else:
 
         def one_source(source, _):

time: 30.8 us -> 30.8 us (level)
  no operation moved by 1% of the time
where the time goes in v1:
time: 30.8 us; the launch traced here: 30.5 us
  blocking collectives  25.2 us (82%)
  Pallas kernels  4.63 us (15%)
  between operations  0.67 us (2%)
    all_to_all x1, blocking collectives, per_device(): lax.all_to_all(send.reshape(devices, height, lanes), ('src', 'tile'), 0, 0)  16.2 us
    all_to_all x1, blocking collectives, per_device(): lax.all_to_all(image.reshape((devices,) + image.shape[2:]), ('src', 'tile...  9.07 us
    pallas_call x1, Pallas kernels, per_device(): pl.pallas_call(functools.partial(image_kernel, rim, comps, rows, ranks),...  2.8 us
    pallas_call x1, Pallas kernels, per_device(): pl.pallas_call(functools.partial(send_kernel, rim), out_shape=jax.ShapeDt...  1.05 us
    pallas_call x1, Pallas kernels, per_device(): pl.pallas_call(merge_kernel, out_shape=jax.ShapeDtypeStruct((1, rows, wid...  0.78 us

profile of v1, /device:TPU:0, one launch (start us, length us, event | category | flops | bytes accessed | tf_op | source)
XLA Modules:
  0.0 30.5 jit_solution(11605563955137522446)
XLA Ops:
  0.7 1.1 %send_columns.1 = bf16[8,2,24,256]{3,2,1,0:T(8,128)(2,1)S(1)} custom-call(bf16[1,8,3,2,512]{4,3,2,1,0:T(2,128)(2,1)} %bitcast.7, bf16[1,2,8,65]{3,2,1,0:T(8,128)(2,1)} %x_taps_hbm.1, bf16[1,2,8,65]{3,2,1,0:T(8,128)(2,1)} %y_taps_hbm.1, f32[1]{0:T(128)S(6)} %copy.5.weight_ref), custom_call_target="tpu_custom_call" | custom-call | tf_op jit(solution)/shard_map/send_columns/pallas_call | solution.py:212
  1.7 16.2 %all_to_all.10 = bf16[16,24,256]{2,1,0:T(8,128)(2,1)S(1)} all-to-all(bf16[16,24,256]{2,1,0:T(8,128)(2,1)S(1)} %bitcast.5), channel_id=1, replica_groups=mesh['group'=2,'src'=8,'tile'=2] {'src','tile'}, dimensions={0} | all-to-all | bytes 393216 | tf_op jit(solution)/shard_map/all_to_all | solution.py:226
  17.9 2.8 %image.1 = f32[8,2,2,128]{3,2,1,0:T(2,128)S(1)} custom-call(bf16[8,2,24,256]{3,2,1,0:T(8,128)(2,1)S(1)} %bitcast.4), custom_call_target="tpu_custom_call" | custom-call | tf_op jit(solution)/shard_map/image/pallas_call | solution.py:228
  20.7 9.1 %all_to_all.11.parts_ref = f32[16,2,128]{2,1,0:T(2,128)S(1)} all-to-all(f32[16,2,128]{2,1,0:T(2,128)S(1)} %bitcast.6), channel_id=1, replica_groups=mesh['group'=2,'src'=8,'tile'=2] {'src','tile'}, dimensions={0} | all-to-all | bytes 32768 | tf_op jit(solution)/shard_map/all_to_all | solution.py:244
  29.8 0.8 %merge_columns.1 = f32[1,8,512]{2,1,0:T(8,128)} custom-call(f32[16,2,128]{2,1,0:T(2,128)S(1)} %all_to_all.11.parts_ref), custom_call_target="tpu_custom_call" | custom-call | tf_op jit(solution)/shard_map/merge_columns/pallas_call | solution.py:245

commit v2 on v1

--- a/solution.py
+++ b/solution.py
@@ -68,12 +68,11 @@
     chunks = slab_rows // LANES
     windows = row_ref.shape[1]
     half_lanes = LANES // 2
-    for tile in range(tiles):
-        cells = got_ref[:, tile].astype(F32)
-        for comp in range(comps):
-            some = cells[:, comp * rows : (comp + 1) * rows, :].reshape(tile_rows, lanes).astype(BF16)
-            at = comp * slab_rows + tile * tile_rows
-            field_ref[at : at + tile_rows, :] = some
+    tile_cells = [got_ref[:, tile].astype(F32) for tile in range(tiles)]
+    for comp in range(comps):
+        lines = [cells[:, comp * rows : (comp + 1) * rows, :].reshape(tile_rows, lanes) for cells in tile_cells]
+        lines = jnp.concatenate(lines, axis=0)
+        field_ref[:, comp * slab_rows : (comp + 1) * slab_rows] = lines.T.astype(BF16)
 
     tap = lax.broadcasted_iota(jnp.int32, (2 * rim, LANES), 0)
     lane = lax.broadcasted_iota(jnp.int32, (2 * rim, LANES), 1)
@@ -120,9 +119,7 @@
                     ).astype(BF16)
 
     def column_pass(slot):
-        passed = lax.dot_general(
-            column_ref[slot].astype(BF16), field_ref[...], (((1,), (1,)), ((), ())), preferred_element_type=F32
-        )
+        passed = jnp.dot(column_ref[slot].astype(BF16), field_ref[...], preferred_element_type=F32)
         for chunk in range(chunks):
             for r in range(ranks):
                 cells = []
@@ -231,7 +228,7 @@
         in_specs=[whole],
         out_specs=whole,
         scratch_shapes=[
-            pltpu.VMEM((comps * slab_rows, lanes), BF16),
+            pltpu.VMEM((lanes, comps * slab_rows), BF16),
             pltpu.VMEM((4, sources * ranks, LANES), F32),
             pltpu.VMEM((slots, 2 * ranks * mine, lanes), BF16 if mine % 16 == 0 else F32),
             pltpu.VMEM((slots, chunks, 2 * comps * mine, ranks * LANES), BF16),

time: 30.8 us -> 30.9 us (level)
  no operation moved by 1% of the time
where the time goes in v2:
time: 30.9 us; the launch traced here: 30.7 us
  blocking collectives  25.2 us (82%)
  Pallas kernels  4.74 us (15%)
  between operations  0.67 us (2%)
    all_to_all x1, blocking collectives, per_device(): lax.all_to_all(send.reshape(devices, height, lanes), ('src', 'tile'), 0, 0)  16.2 us
    all_to_all x1, blocking collectives, per_device(): lax.all_to_all(image.reshape((devices,) + image.shape[2:]), ('src', 'tile...  9.07 us
    pallas_call x1, Pallas kernels, per_device(): pl.pallas_call(functools.partial(image_kernel, rim, comps, rows, ranks),...  2.91 us
    pallas_call x1, Pallas kernels, per_device(): pl.pallas_call(functools.partial(send_kernel, rim), out_shape=jax.ShapeDt...  1.05 us
    pallas_call x1, Pallas kernels, per_device(): pl.pallas_call(merge_kernel, out_shape=jax.ShapeDtypeStruct((1, rows, wid...  0.78 us

profile of v2, /device:TPU:0, one launch (start us, length us, event | category | flops | bytes accessed | tf_op | source)
XLA Modules:
  0.0 30.7 jit_solution(16445797134747866698)
XLA Ops:
  0.7 1.1 %send_columns.1 = bf16[8,2,24,256]{3,2,1,0:T(8,128)(2,1)S(1)} custom-call(bf16[1,8,3,2,512]{4,3,2,1,0:T(2,128)(2,1)} %bitcast.7, bf16[1,2,8,65]{3,2,1,0:T(8,128)(2,1)} %x_taps_hbm.1, bf16[1,2,8,65]{3,2,1,0:T(8,128)(2,1)} %y_taps_hbm.1, f32[1]{0:T(128)S(6)} %copy.5.weight_ref), custom_call_target="tpu_custom_call" | custom-call | tf_op jit(solution)/shard_map/send_columns/pallas_call | solution.py:209
  1.7 16.2 %all_to_all.10 = bf16[16,24,256]{2,1,0:T(8,128)(2,1)S(1)} all-to-all(bf16[16,24,256]{2,1,0:T(8,128)(2,1)S(1)} %bitcast.5), channel_id=1, replica_groups=mesh['group'=2,'src'=8,'tile'=2] {'src','tile'}, dimensions={0} | all-to-all | bytes 393216 | tf_op jit(solution)/shard_map/all_to_all | solution.py:223
  17.9 2.9 %image.1 = f32[8,2,2,128]{3,2,1,0:T(2,128)S(1)} custom-call(bf16[8,2,24,256]{3,2,1,0:T(8,128)(2,1)S(1)} %bitcast.4), custom_call_target="tpu_custom_call" | custom-call | tf_op jit(solution)/shard_map/image/pallas_call | solution.py:225
  20.8 9.1 %all_to_all.11.parts_ref = f32[16,2,128]{2,1,0:T(2,128)S(1)} all-to-all(f32[16,2,128]{2,1,0:T(2,128)S(1)} %bitcast.6), channel_id=1, replica_groups=mesh['group'=2,'src'=8,'tile'=2] {'src','tile'}, dimensions={0} | all-to-all | bytes 32768 | tf_op jit(solution)/shard_map/all_to_all | solution.py:241
  29.9 0.8 %merge_columns.1 = f32[1,8,512]{2,1,0:T(8,128)} custom-call(f32[16,2,128]{2,1,0:T(2,128)S(1)} %all_to_all.11.parts_ref), custom_call_target="tpu_custom_call" | custom-call | tf_op jit(solution)/shard_map/merge_columns/pallas_call | solution.py:242

commit v3 on v1

--- a/solution.py
+++ b/solution.py
@@ -22,7 +22,7 @@
     for copy in copies:
         copy.wait()
     _, rows, comps, _, width = field_ref.shape
-    sources, tiles, height, lanes = send_ref.shape
+    tiles, sources, height, lanes = send_ref.shape
     ranks, taps = x_taps_ref.shape[2:]
     mine = width // (sources * tiles)
     window = mine + 2 * rim
@@ -52,8 +52,8 @@
         for part in range(2):
             plane = [padded[comp][part][:, at : at + window] for comp in range(comps)]
             cells += [jnp.concatenate(plane, axis=0), spares[part]]
-        source, tile = divmod(device, tiles)
-        send_ref[source, tile] = jnp.concatenate(cells, axis=1).astype(BF16)
+        tile, source = divmod(device, sources)
+        send_ref[tile, source] = jnp.concatenate(cells, axis=1).astype(BF16)
 
 
 def rolled(line, count):
@@ -61,7 +61,7 @@
 
 
 def image_kernel(rim, comps, rows, ranks, got_ref, out_ref, field_ref, taps_ref, column_ref, lhs_ref, row_ref, total_ref):
-    sources, tiles, _, lanes = got_ref.shape
+    tiles, sources, _, lanes = got_ref.shape
     mine, slab_rows = total_ref.shape
     window = mine + 2 * rim
     tile_rows = sources * rows
@@ -69,7 +69,7 @@
     windows = row_ref.shape[1]
     half_lanes = LANES // 2
     for tile in range(tiles):
-        cells = got_ref[:, tile].astype(F32)
+        cells = got_ref[tile].astype(F32)
         for comp in range(comps):
             some = cells[:, comp * rows : (comp + 1) * rows, :].reshape(tile_rows, lanes).astype(BF16)
             at = comp * slab_rows + tile * tile_rows
@@ -82,7 +82,7 @@
     x_last = (lane[:1] == 2 * rim).astype(F32)
     y_last = (lane[:1] == LANES - rim).astype(F32)
     for n, (place, last_place) in enumerate(((x_place, x_last), (y_place, y_last))):
-        block = got_ref[:, n].astype(F32)
+        block = got_ref[n].astype(F32)
         taps = jnp.concatenate([block[:, :, LANES - rim : LANES], block[:, :, 2 * LANES - rim :]], axis=2)
         for part in range(2):
             first = taps[:, part * ranks : (part + 1) * ranks].reshape(sources * ranks, 2 * rim)
@@ -133,7 +133,7 @@
                 lhs_ref[slot, chunk, :, r * LANES : (r + 1) * LANES] = jnp.concatenate(cells, axis=0).astype(BF16)
 
     def row_pass(source, slot):
-        weight = got_ref[source, 0].astype(F32)[2 * ranks : 2 * ranks + 1, LANES - rim : LANES]
+        weight = got_ref[0, source].astype(F32)[2 * ranks : 2 * ranks + 1, LANES - rim : LANES]
         weight = weight[:, 2:3] + weight[:, 3:4] + weight[:, 4:5]
         for chunk in range(chunks):
             image = None
@@ -176,7 +176,7 @@
             block = lines[piece * rows : (piece + 1) * rows]
             step = out_ref.shape[2]
             groups = [block[n : n + step] for n in range(0, rows, step)]
-            out_ref[source, tile] = jnp.concatenate(groups, axis=1)
+            out_ref[tile, source] = jnp.concatenate(groups, axis=1)
 
 
 def merge_kernel(parts_ref, out_ref):
@@ -211,7 +211,7 @@
 
     send = pl.pallas_call(
         functools.partial(send_kernel, rim),
-        out_shape=jax.ShapeDtypeStruct((sources, tiles, height, lanes), BF16),
+        out_shape=jax.ShapeDtypeStruct((tiles, sources, height, lanes), BF16),
         in_specs=[pl.BlockSpec(memory_space=pltpu.HBM)] * 3 + [pl.BlockSpec(memory_space=pltpu.SMEM)],
         out_specs=whole,
         scratch_shapes=[
@@ -223,11 +223,11 @@
         compiler_params=params,
         name="send_columns",
     )(in_hbm(near_field.transpose(0, 1, 3, 2, 4)), in_hbm(x_taps), in_hbm(y_taps), source_weight)
-    got = lax.all_to_all(send.reshape(devices, height, lanes), ("src", "tile"), 0, 0).reshape(send.shape)
+    got = lax.all_to_all(send.reshape(devices, height, lanes), ("tile", "src"), 0, 0).reshape(send.shape)
     slots = sources if sources <= 8 else 1
     image = pl.pallas_call(
         functools.partial(image_kernel, rim, comps, rows, ranks),
-        out_shape=jax.ShapeDtypeStruct((sources, tiles, step, rows // step * mine), F32),
+        out_shape=jax.ShapeDtypeStruct((tiles, sources, step, rows // step * mine), F32),
         in_specs=[whole],
         out_specs=whole,
         scratch_shapes=[
@@ -241,7 +241,7 @@
         compiler_params=params,
         name="image",
     )(got)
-    parts = lax.all_to_all(image.reshape((devices,) + image.shape[2:]), ("src", "tile"), 0, 0)
+    parts = lax.all_to_all(image.reshape((devices,) + image.shape[2:]), ("tile", "src"), 0, 0)
     return pl.pallas_call(
         merge_kernel,
         out_shape=jax.ShapeDtypeStruct((1, rows, width), F32),

time: 30.8 us -> 30.7 us (level)
  no operation moved by 1% of the time
where the time goes in v3:
time: 30.7 us; the launch traced here: 30.5 us
  blocking collectives  25.2 us (82%)
  Pallas kernels  4.63 us (15%)
  between operations  0.67 us (2%)
    all_to_all x1, blocking collectives, per_device(): lax.all_to_all(send.reshape(devices, height, lanes), ('tile', 'src'), 0, 0)  16.2 us
    all_to_all x1, blocking collectives, per_device(): lax.all_to_all(image.reshape((devices,) + image.shape[2:]), ('tile', 'src...  8.99 us
    pallas_call x1, Pallas kernels, per_device(): pl.pallas_call(functools.partial(image_kernel, rim, comps, rows, ranks),...  2.8 us
    pallas_call x1, Pallas kernels, per_device(): pl.pallas_call(functools.partial(send_kernel, rim), out_shape=jax.ShapeDt...  1.05 us
    pallas_call x1, Pallas kernels, per_device(): pl.pallas_call(merge_kernel, out_shape=jax.ShapeDtypeStruct((1, rows, wid...  0.78 us

profile of v3, /device:TPU:0, one launch (start us, length us, event | category | flops | bytes accessed | tf_op | source)
XLA Modules:
  0.0 30.5 jit_solution(1481462345352721044)
XLA Ops:
  0.7 1.1 %send_columns.1 = bf16[2,8,24,256]{3,2,1,0:T(8,128)(2,1)S(1)} custom-call(bf16[1,8,3,2,512]{4,3,2,1,0:T(2,128)(2,1)} %bitcast.7, bf16[1,2,8,65]{3,2,1,0:T(8,128)(2,1)} %x_taps_hbm.1, bf16[1,2,8,65]{3,2,1,0:T(8,128)(2,1)} %y_taps_hbm.1, f32[1]{0:T(128)S(6)} %copy.5.weight_ref), custom_call_target="tpu_custom_call" | custom-call | tf_op jit(solution)/shard_map/send_columns/pallas_call | solution.py:212
  1.7 16.2 %all_to_all.10 = bf16[16,24,256]{2,1,0:T(8,128)(2,1)S(1)} all-to-all(bf16[16,24,256]{2,1,0:T(8,128)(2,1)S(1)} %bitcast.5), channel_id=1, replica_groups=mesh['group'=2,'src'=8,'tile'=2] {'tile','src'}, dimensions={0} | all-to-all | bytes 393216 | tf_op jit(solution)/shard_map/all_to_all | solution.py:226
  17.9 2.8 %image.1 = f32[2,8,2,128]{3,2,1,0:T(2,128)S(1)} custom-call(bf16[2,8,24,256]{3,2,1,0:T(8,128)(2,1)S(1)} %bitcast.4), custom_call_target="tpu_custom_call" | custom-call | tf_op jit(solution)/shard_map/image/pallas_call | solution.py:228
  20.7 9.0 %all_to_all.11.parts_ref = f32[16,2,128]{2,1,0:T(2,128)S(1)} all-to-all(f32[16,2,128]{2,1,0:T(2,128)S(1)} %bitcast.6), channel_id=1, replica_groups=mesh['group'=2,'src'=8,'tile'=2] {'tile','src'}, dimensions={0} | all-to-all | bytes 32768 | tf_op jit(solution)/shard_map/all_to_all | solution.py:244
  29.7 0.8 %merge_columns.1 = f32[1,8,512]{2,1,0:T(8,128)} custom-call(f32[16,2,128]{2,1,0:T(2,128)S(1)} %all_to_all.11.parts_ref), custom_call_target="tpu_custom_call" | custom-call | tf_op jit(solution)/shard_map/merge_columns/pallas_call | solution.py:245

commit v4 on v1

--- a/solution.py
+++ b/solution.py
@@ -119,18 +119,24 @@
                         band, axis=0
                     ).astype(BF16)
 
-    def column_pass(slot):
+    def column_pass(slot, count):
+        height = 2 * ranks * mine
         passed = lax.dot_general(
-            column_ref[slot].astype(BF16), field_ref[...], (((1,), (1,)), ((), ())), preferred_element_type=F32
+            column_ref[slot : slot + count].reshape(count * height, lanes).astype(BF16),
+            field_ref[...],
+            (((1,), (1,)), ((), ())),
+            preferred_element_type=F32,
         )
-        for chunk in range(chunks):
-            for r in range(ranks):
-                cells = []
-                for part in range(2):
-                    for comp in range(comps):
-                        top, left = (2 * r + part) * mine, comp * slab_rows + chunk * LANES
-                        cells.append(passed[top : top + mine, left : left + LANES])
-                lhs_ref[slot, chunk, :, r * LANES : (r + 1) * LANES] = jnp.concatenate(cells, axis=0).astype(BF16)
+        for n in range(count):
+            for chunk in range(chunks):
+                for r in range(ranks):
+                    cells = []
+                    for part in range(2):
+                        for comp in range(comps):
+                            top, left = n * height + (2 * r + part) * mine, comp * slab_rows + chunk * LANES
+                            cells.append(passed[top : top + mine, left : left + LANES])
+                    cells = jnp.concatenate(cells, axis=0).astype(BF16)
+                    lhs_ref[slot + n, chunk, :, r * LANES : (r + 1) * LANES] = cells
 
     def row_pass(source, slot):
         weight = got_ref[source, 0].astype(F32)[2 * ranks : 2 * ranks + 1, LANES - rim : LANES]
@@ -152,20 +158,27 @@
             total_ref[:, chunk * LANES : (chunk + 1) * LANES] += weight * power
 
     if sources <= 8:
-        bands(0, 0)
-        column_pass(0)
-        bands(1, 1)
-        for source in range(sources):
-            if source + 1 < sources:
-                column_pass(source + 1)
-            if source + 2 < sources:
-                bands(source + 2, source + 2)
-            row_pass(source, source)
+        count = 2 if sources % 2 == 0 else 1
+        steps = list(range(0, sources, count))
+
+        def prepare(step):
+            for source in range(step, min(step + count, sources)):
+                bands(source, source)
+
+        prepare(0)
+        column_pass(0, count)
+        prepare(count)
+        for step in steps:
+            if step + count < sources:
+                column_pass(step + count, count)
+            prepare(step + 2 * count)
+            for source in range(step, step + count):
+                row_pass(source, source)
     else:
 
         def one_source(source, _):
             bands(source, 0)
-            column_pass(0)
+            column_pass(0, 1)
             row_pass(source, 0)
 
         lax.fori_loop(0, sources, one_source, None)

time: 30.8 us -> 30.9 us (level)
  no operation moved by 1% of the time
where the time goes in v4:
time: 30.9 us; the launch traced here: 30.7 us
  blocking collectives  25.2 us (82%)
  Pallas kernels  4.79 us (16%)
  between operations  0.67 us (2%)
    all_to_all x1, blocking collectives, per_device(): lax.all_to_all(send.reshape(devices, height, lanes), ('src', 'tile'), 0, 0)  16.2 us
    all_to_all x1, blocking collectives, per_device(): lax.all_to_all(image.reshape((devices,) + image.shape[2:]), ('src', 'tile...  9.07 us
    pallas_call x1, Pallas kernels, per_device(): pl.pallas_call(functools.partial(image_kernel, rim, comps, rows, ranks),...  2.96 us
    pallas_call x1, Pallas kernels, per_device(): pl.pallas_call(functools.partial(send_kernel, rim), out_shape=jax.ShapeDt...  1.05 us
    pallas_call x1, Pallas kernels, per_device(): pl.pallas_call(merge_kernel, out_shape=jax.ShapeDtypeStruct((1, rows, wid...  0.78 us

profile of v4, /device:TPU:0, one launch (start us, length us, event | category | flops | bytes accessed | tf_op | source)
XLA Modules:
  0.0 30.7 jit_solution(16695286953491142321)
XLA Ops:
  0.7 1.1 %send_columns.1 = bf16[8,2,24,256]{3,2,1,0:T(8,128)(2,1)S(1)} custom-call(bf16[1,8,3,2,512]{4,3,2,1,0:T(2,128)(2,1)} %bitcast.7, bf16[1,2,8,65]{3,2,1,0:T(8,128)(2,1)} %x_taps_hbm.1, bf16[1,2,8,65]{3,2,1,0:T(8,128)(2,1)} %y_taps_hbm.1, f32[1]{0:T(128)S(6)} %copy.5.weight_ref), custom_call_target="tpu_custom_call" | custom-call | tf_op jit(solution)/shard_map/send_columns/pallas_call | solution.py:225
  1.7 16.2 %all_to_all.10 = bf16[16,24,256]{2,1,0:T(8,128)(2,1)S(1)} all-to-all(bf16[16,24,256]{2,1,0:T(8,128)(2,1)S(1)} %bitcast.5), channel_id=1, replica_groups=mesh['group'=2,'src'=8,'tile'=2] {'src','tile'}, dimensions={0} | all-to-all | bytes 393216 | tf_op jit(solution)/shard_map/all_to_all | solution.py:239
  17.9 3.0 %image.1 = f32[8,2,2,128]{3,2,1,0:T(2,128)S(1)} custom-call(bf16[8,2,24,256]{3,2,1,0:T(8,128)(2,1)S(1)} %bitcast.4), custom_call_target="tpu_custom_call" | custom-call | tf_op jit(solution)/shard_map/image/pallas_call | solution.py:241
  20.9 9.1 %all_to_all.11.parts_ref = f32[16,2,128]{2,1,0:T(2,128)S(1)} all-to-all(f32[16,2,128]{2,1,0:T(2,128)S(1)} %bitcast.6), channel_id=1, replica_groups=mesh['group'=2,'src'=8,'tile'=2] {'src','tile'}, dimensions={0} | all-to-all | bytes 32768 | tf_op jit(solution)/shard_map/all_to_all | solution.py:257
  29.9 0.8 %merge_columns.1 = f32[1,8,512]{2,1,0:T(8,128)} custom-call(f32[16,2,128]{2,1,0:T(2,128)S(1)} %all_to_all.11.parts_ref), custom_call_target="tpu_custom_call" | custom-call | tf_op jit(solution)/shard_map/merge_columns/pallas_call | solution.py:258

commit v5 on v0

--- a/solution.py
+++ b/solution.py
@@ -93,6 +93,7 @@
     i = lax.broadcasted_iota(jnp.int32, (LANES, LANES), 1)
     near = jnp.abs(i - k) < half_lanes
     masks = [near] if windows == 1 else [k - i > half_lanes, near, k - i < -half_lanes]
+    masks = [jnp.where(mask, 1.0, 0.0).astype(BF16) for mask in masks]
     total_ref[...] = jnp.zeros_like(total_ref)
 
     def bands(source, slot):
@@ -108,11 +109,17 @@
             column_ref[slot, top + mine : top + 2 * mine, LANES:] = re.astype(column_ref.dtype)
         for r in range(ranks):
             for part in range(2):
-                ring = rolled(y_lines[part][r : r + 1], LANES)
-                for n, mask in enumerate(masks):
-                    row_ref[slot, n, r * LANES : (r + 1) * LANES, part * LANES : (part + 1) * LANES] = jnp.where(
-                        mask, ring, 0.0
-                    ).astype(BF16)
+                base = rolled(y_lines[part][r : r + 1], 16).astype(BF16)
+                for top in range(0, LANES, 16):
+                    block = pltpu.roll(base, top, 1) if top > 0 else base
+                    inner = rim <= top < LANES - rim
+                    for n, mask in enumerate(masks):
+                        if not inner:
+                            cells = block * mask[top : top + 16]
+                        else:
+                            cells = block if n == windows // 2 else jnp.zeros_like(block)
+                        at = r * LANES + top
+                        row_ref[slot, n, at : at + 16, part * LANES : (part + 1) * LANES] = cells
 
     def column_pass(slot):
         passed = lax.dot_general(
@@ -153,9 +160,9 @@
         for source in range(sources):
             if source + 1 < sources:
                 column_pass(source + 1)
-            row_pass(source, source)
             if source + 2 < sources:
                 bands(source + 2, source + 2)
+            row_pass(source, source)
     else:
 
         def one_source(source, _):

time: 30.8 us -> 32.7 us (1.062)
  Pallas kernels: 4.64 us -> 6.5 us
    pallas_call x1, Pallas kernels: 2.81 us -> 4.67 us  [per_device(): pl.pallas_call(functools.partial(image_kernel, rim, comps, rows, ranks),...]
where the time goes in v5:
time: 32.7 us; the launch traced here: 32.4 us
  blocking collectives  25.2 us (77%)
  Pallas kernels  6.5 us (20%)
  between operations  0.67 us (2%)
    all_to_all x1, blocking collectives, per_device(): lax.all_to_all(send.reshape(devices, height, lanes), ('src', 'tile'), 0, 0)  16.2 us
    all_to_all x1, blocking collectives, per_device(): lax.all_to_all(image.reshape((devices,) + image.shape[2:]), ('src', 'tile...  9.07 us
    pallas_call x1, Pallas kernels, per_device(): pl.pallas_call(functools.partial(image_kernel, rim, comps, rows, ranks),...  4.67 us
    pallas_call x1, Pallas kernels, per_device(): pl.pallas_call(functools.partial(send_kernel, rim), out_shape=jax.ShapeDt...  1.05 us
    pallas_call x1, Pallas kernels, per_device(): pl.pallas_call(merge_kernel, out_shape=jax.ShapeDtypeStruct((1, rows, wid...  0.78 us

profile of v5, /device:TPU:0, one launch (start us, length us, event | category | flops | bytes accessed | tf_op | source)
XLA Modules:
  0.0 32.4 jit_solution(12200221639091566177)
XLA Ops:
  0.7 1.1 %send_columns.1 = bf16[8,2,24,256]{3,2,1,0:T(8,128)(2,1)S(1)} custom-call(bf16[1,8,3,2,512]{4,3,2,1,0:T(2,128)(2,1)} %bitcast.7, bf16[1,2,8,65]{3,2,1,0:T(8,128)(2,1)} %x_taps_hbm.1, bf16[1,2,8,65]{3,2,1,0:T(8,128)(2,1)} %y_taps_hbm.1, f32[1]{0:T(128)S(6)} %copy.5.weight_ref), custom_call_target="tpu_custom_call" | custom-call | tf_op jit(solution)/shard_map/send_columns/pallas_call | solution.py:214
  1.7 16.2 %all_to_all.10 = bf16[16,24,256]{2,1,0:T(8,128)(2,1)S(1)} all-to-all(bf16[16,24,256]{2,1,0:T(8,128)(2,1)S(1)} %bitcast.5), channel_id=1, replica_groups=mesh['group'=2,'src'=8,'tile'=2] {'src','tile'}, dimensions={0} | all-to-all | bytes 393216 | tf_op jit(solution)/shard_map/all_to_all | solution.py:228
  17.9 4.7 %image.1 = f32[8,2,2,128]{3,2,1,0:T(2,128)S(1)} custom-call(bf16[8,2,24,256]{3,2,1,0:T(8,128)(2,1)S(1)} %bitcast.4), custom_call_target="tpu_custom_call" | custom-call | tf_op jit(solution)/shard_map/image/pallas_call | solution.py:230
  22.6 9.1 %all_to_all.11.parts_ref = f32[16,2,128]{2,1,0:T(2,128)S(1)} all-to-all(f32[16,2,128]{2,1,0:T(2,128)S(1)} %bitcast.6), channel_id=1, replica_groups=mesh['group'=2,'src'=8,'tile'=2] {'src','tile'}, dimensions={0} | all-to-all | bytes 32768 | tf_op jit(solution)/shard_map/all_to_all | solution.py:246
  31.6 0.8 %merge_columns.1 = f32[1,8,512]{2,1,0:T(8,128)} custom-call(f32[16,2,128]{2,1,0:T(2,128)S(1)} %all_to_all.11.parts_ref), custom_call_target="tpu_custom_call" | custom-call | tf_op jit(solution)/shard_map/merge_columns/pallas_call | solution.py:247

commit v6 on v0

--- a/solution.py
+++ b/solution.py
@@ -106,13 +106,18 @@
             column_ref[slot, top : top + mine, LANES:] = (-im).astype(column_ref.dtype)
             column_ref[slot, top + mine : top + 2 * mine, :LANES] = im.astype(column_ref.dtype)
             column_ref[slot, top + mine : top + 2 * mine, LANES:] = re.astype(column_ref.dtype)
-        for r in range(ranks):
-            for part in range(2):
-                ring = rolled(y_lines[part][r : r + 1], LANES)
-                for n, mask in enumerate(masks):
-                    row_ref[slot, n, r * LANES : (r + 1) * LANES, part * LANES : (part + 1) * LANES] = jnp.where(
-                        mask, ring, 0.0
-                    ).astype(BF16)
+        for part in range(2):
+            wide = jnp.broadcast_to(y_lines[part][:, None, :], (ranks, LANES, LANES))
+            rings = pltpu.roll(wide, 0, 2, stride=1, stride_axis=1)
+            for n, mask in enumerate(masks):
+                middle = rings[:, rim : LANES - rim] if n == windows // 2 else jnp.zeros((ranks, LANES - 2 * rim, LANES), F32)
+                band = [
+                    jnp.where(mask[None, :rim], rings[:, :rim], 0.0),
+                    middle,
+                    jnp.where(mask[None, LANES - rim :], rings[:, LANES - rim :], 0.0),
+                ]
+                band = jnp.concatenate(band, axis=1).reshape(ranks * LANES, LANES)
+                row_ref[slot, n, :, part * LANES : (part + 1) * LANES] = band.astype(BF16)
 
     def column_pass(slot):
         passed = lax.dot_general(
@@ -153,9 +158,9 @@
         for source in range(sources):
             if source + 1 < sources:
                 column_pass(source + 1)
-            row_pass(source, source)
             if source + 2 < sources:
                 bands(source + 2, source + 2)
+            row_pass(source, source)
     else:
 
         def one_source(source, _):

time: 30.8 us -> 30.8 us (level)
  no operation moved by 1% of the time
where the time goes in v6:
time: 30.8 us; the launch traced here: 30.6 us
  blocking collectives  25.2 us (82%)
  Pallas kernels  4.67 us (15%)
  between operations  0.67 us (2%)
    all_to_all x1, blocking collectives, per_device(): lax.all_to_all(send.reshape(devices, height, lanes), ('src', 'tile'), 0, 0)  16.2 us
    all_to_all x1, blocking collectives, per_device(): lax.all_to_all(image.reshape((devices,) + image.shape[2:]), ('src', 'tile...  9.07 us
    pallas_call x1, Pallas kernels, per_device(): pl.pallas_call(functools.partial(image_kernel, rim, comps, rows, ranks),...  2.85 us
    pallas_call x1, Pallas kernels, per_device(): pl.pallas_call(functools.partial(send_kernel, rim), out_shape=jax.ShapeDt...  1.05 us
    pallas_call x1, Pallas kernels, per_device(): pl.pallas_call(merge_kernel, out_shape=jax.ShapeDtypeStruct((1, rows, wid...  0.78 us

profile of v6, /device:TPU:0, one launch (start us, length us, event | category | flops | bytes accessed | tf_op | source)
XLA Modules:
  0.0 30.6 jit_solution(7319101837975024730)
XLA Ops:
  0.7 1.1 %send_columns.1 = bf16[8,2,24,256]{3,2,1,0:T(8,128)(2,1)S(1)} custom-call(bf16[1,8,3,2,512]{4,3,2,1,0:T(2,128)(2,1)} %bitcast.7, bf16[1,2,8,65]{3,2,1,0:T(8,128)(2,1)} %x_taps_hbm.1, bf16[1,2,8,65]{3,2,1,0:T(8,128)(2,1)} %y_taps_hbm.1, f32[1]{0:T(128)S(6)} %copy.5.weight_ref), custom_call_target="tpu_custom_call" | custom-call | tf_op jit(solution)/shard_map/send_columns/pallas_call | solution.py:212
  1.7 16.2 %all_to_all.10 = bf16[16,24,256]{2,1,0:T(8,128)(2,1)S(1)} all-to-all(bf16[16,24,256]{2,1,0:T(8,128)(2,1)S(1)} %bitcast.5), channel_id=1, replica_groups=mesh['group'=2,'src'=8,'tile'=2] {'src','tile'}, dimensions={0} | all-to-all | bytes 393216 | tf_op jit(solution)/shard_map/all_to_all | solution.py:226
  17.9 2.8 %image.1 = f32[8,2,2,128]{3,2,1,0:T(2,128)S(1)} custom-call(bf16[8,2,24,256]{3,2,1,0:T(8,128)(2,1)S(1)} %bitcast.4), custom_call_target="tpu_custom_call" | custom-call | tf_op jit(solution)/shard_map/image/pallas_call | solution.py:228
  20.7 9.1 %all_to_all.11.parts_ref = f32[16,2,128]{2,1,0:T(2,128)S(1)} all-to-all(f32[16,2,128]{2,1,0:T(2,128)S(1)} %bitcast.6), channel_id=1, replica_groups=mesh['group'=2,'src'=8,'tile'=2] {'src','tile'}, dimensions={0} | all-to-all | bytes 32768 | tf_op jit(solution)/shard_map/all_to_all | solution.py:244
  29.8 0.8 %merge_columns.1 = f32[1,8,512]{2,1,0:T(8,128)} custom-call(f32[16,2,128]{2,1,0:T(2,128)S(1)} %all_to_all.11.parts_ref), custom_call_target="tpu_custom_call" | custom-call | tf_op jit(solution)/shard_map/merge_columns/pallas_call | solution.py:245

commit v7 on v1

--- a/solution.py
+++ b/solution.py
@@ -19,18 +19,13 @@
     copies = [pltpu.make_async_copy(source, target, sems.at[n]) for n, (source, target) in enumerate(pairs)]
     for copy in copies:
         copy.start()
-    for copy in copies:
-        copy.wait()
+    copies[1].wait()
+    copies[2].wait()
     _, rows, comps, _, width = field_ref.shape
     sources, tiles, height, lanes = send_ref.shape
     ranks, taps = x_taps_ref.shape[2:]
     mine = width // (sources * tiles)
     window = mine + 2 * rim
-    edge = jnp.zeros((rows, rim), F32)
-    field = field_ref[0].astype(F32)
-    padded = [
-        [jnp.concatenate([edge, field[:, comp, part, :], edge], axis=1) for part in range(2)] for comp in range(comps)
-    ]
     lower = lax.axis_index("tile") == 0
     lines = [
         jnp.where(lower, x_taps_ref[0, part].astype(F32), y_taps_ref[0, part].astype(F32)) for part in range(2)
@@ -46,6 +41,12 @@
     if window < LANES - rim:
         gap = jnp.zeros((height, LANES - rim - window), F32)
         spares = [jnp.concatenate([gap, part], axis=1) for part in spares]
+    copies[0].wait()
+    edge = jnp.zeros((rows, rim), F32)
+    field = field_ref[0].astype(F32)
+    padded = [
+        [jnp.concatenate([edge, field[:, comp, part, :], edge], axis=1) for part in range(2)] for comp in range(comps)
+    ]
     for device in range(sources * tiles):
         at = device * mine
         cells = []

time: 30.8 us -> 30.8 us (level)
  no operation moved by 1% of the time
where the time goes in v7:
time: 30.8 us; the launch traced here: 30.6 us
  blocking collectives  25.2 us (82%)
  Pallas kernels  4.64 us (15%)
  between operations  0.67 us (2%)
    all_to_all x1, blocking collectives, per_device(): lax.all_to_all(send.reshape(devices, height, lanes), ('src', 'tile'), 0, 0)  16.2 us
    all_to_all x1, blocking collectives, per_device(): lax.all_to_all(image.reshape((devices,) + image.shape[2:]), ('src', 'tile...  9.07 us
    pallas_call x1, Pallas kernels, per_device(): pl.pallas_call(functools.partial(image_kernel, rim, comps, rows, ranks),...  2.81 us
    pallas_call x1, Pallas kernels, per_device(): pl.pallas_call(functools.partial(send_kernel, rim), out_shape=jax.ShapeDt...  1.05 us
    pallas_call x1, Pallas kernels, per_device(): pl.pallas_call(merge_kernel, out_shape=jax.ShapeDtypeStruct((1, rows, wid...  0.78 us

profile of v7, /device:TPU:0, one launch (start us, length us, event | category | flops | bytes accessed | tf_op | source)
XLA Modules:
  0.0 30.6 jit_solution(14032902272184512655)
XLA Ops:
  0.7 1.0 %send_columns.1 = bf16[8,2,24,256]{3,2,1,0:T(8,128)(2,1)S(1)} custom-call(bf16[1,8,3,2,512]{4,3,2,1,0:T(2,128)(2,1)} %bitcast.7, bf16[1,2,8,65]{3,2,1,0:T(8,128)(2,1)} %x_taps_hbm.1, bf16[1,2,8,65]{3,2,1,0:T(8,128)(2,1)} %y_taps_hbm.1, f32[1]{0:T(128)S(6)} %copy.5.weight_ref), custom_call_target="tpu_custom_call" | custom-call | tf_op jit(solution)/shard_map/send_columns/pallas_call | solution.py:213
  1.7 16.2 %all_to_all.10 = bf16[16,24,256]{2,1,0:T(8,128)(2,1)S(1)} all-to-all(bf16[16,24,256]{2,1,0:T(8,128)(2,1)S(1)} %bitcast.5), channel_id=1, replica_groups=mesh['group'=2,'src'=8,'tile'=2] {'src','tile'}, dimensions={0} | all-to-all | bytes 393216 | tf_op jit(solution)/shard_map/all_to_all | solution.py:227
  17.9 2.8 %image.1 = f32[8,2,2,128]{3,2,1,0:T(2,128)S(1)} custom-call(bf16[8,2,24,256]{3,2,1,0:T(8,128)(2,1)S(1)} %bitcast.4), custom_call_target="tpu_custom_call" | custom-call | tf_op jit(solution)/shard_map/image/pallas_call | solution.py:229
  20.7 9.1 %all_to_all.11.parts_ref = f32[16,2,128]{2,1,0:T(2,128)S(1)} all-to-all(f32[16,2,128]{2,1,0:T(2,128)S(1)} %bitcast.6), channel_id=1, replica_groups=mesh['group'=2,'src'=8,'tile'=2] {'src','tile'}, dimensions={0} | all-to-all | bytes 32768 | tf_op jit(solution)/shard_map/all_to_all | solution.py:245
  29.8 0.8 %merge_columns.1 = f32[1,8,512]{2,1,0:T(8,128)} custom-call(f32[16,2,128]{2,1,0:T(2,128)S(1)} %all_to_all.11.parts_ref), custom_call_target="tpu_custom_call" | custom-call | tf_op jit(solution)/shard_map/merge_columns/pallas_call | solution.py:246

commit v8 on v1

--- a/solution.py
+++ b/solution.py
@@ -181,7 +181,22 @@
 
 def merge_kernel(parts_ref, out_ref):
     devices = parts_ref.shape[0]
+    rows = out_ref.shape[1]
     mine = out_ref.shape[2] // devices
+    _, step, held = parts_ref.shape
+    count = rows // step
+    if held == LANES and LANES // mine == count:
+        row_group = lax.broadcasted_iota(jnp.int32, (rows, LANES), 0) // step
+        lane_group = lax.broadcasted_iota(jnp.int32, (rows, LANES), 1) // mine
+        apart = (row_group - lane_group + count) % count
+        for first in range(0, devices, count):
+            cells = jnp.concatenate([parts_ref[first + n] for n in range(count)], axis=0)
+            block = cells
+            for k in range(1, count):
+                moved = pltpu.roll(pltpu.roll(cells, k * step, 0), LANES - k * mine, 1)
+                block = jnp.where(apart == k, moved, block)
+            out_ref[0, :, first * mine : (first + count) * mine] = block
+        return
     blocks = []
     for device in range(devices):
         part = parts_ref[device]

time: 30.8 us -> 30.7 us (level)
  no operation moved by 1% of the time
where the time goes in v8:
time: 30.7 us; the launch traced here: 30.5 us
  blocking collectives  25.2 us (82%)
  Pallas kernels  4.54 us (15%)
  between operations  0.67 us (2%)
    all_to_all x1, blocking collectives, per_device(): lax.all_to_all(send.reshape(devices, height, lanes), ('src', 'tile'), 0, 0)  16.2 us
    all_to_all x1, blocking collectives, per_device(): lax.all_to_all(image.reshape((devices,) + image.shape[2:]), ('src', 'tile...  9.07 us
    pallas_call x1, Pallas kernels, per_device(): pl.pallas_call(functools.partial(image_kernel, rim, comps, rows, ranks),...  2.8 us
    pallas_call x1, Pallas kernels, per_device(): pl.pallas_call(functools.partial(send_kernel, rim), out_shape=jax.ShapeDt...  1.05 us
    pallas_call x1, Pallas kernels, per_device(): pl.pallas_call(merge_kernel, out_shape=jax.ShapeDtypeStruct((1, rows, wid...  0.69 us

profile of v8, /device:TPU:0, one launch (start us, length us, event | category | flops | bytes accessed | tf_op | source)
XLA Modules:
  0.0 30.5 jit_solution(9452556884030933869)
XLA Ops:
  0.7 1.1 %send_columns.1 = bf16[8,2,24,256]{3,2,1,0:T(8,128)(2,1)S(1)} custom-call(bf16[1,8,3,2,512]{4,3,2,1,0:T(2,128)(2,1)} %bitcast.7, bf16[1,2,8,65]{3,2,1,0:T(8,128)(2,1)} %x_taps_hbm.1, bf16[1,2,8,65]{3,2,1,0:T(8,128)(2,1)} %y_taps_hbm.1, f32[1]{0:T(128)S(6)} %copy.5.weight_ref), custom_call_target="tpu_custom_call" | custom-call | tf_op jit(solution)/shard_map/send_columns/pallas_call | solution.py:227
  1.7 16.2 %all_to_all.10 = bf16[16,24,256]{2,1,0:T(8,128)(2,1)S(1)} all-to-all(bf16[16,24,256]{2,1,0:T(8,128)(2,1)S(1)} %bitcast.5), channel_id=1, replica_groups=mesh['group'=2,'src'=8,'tile'=2] {'src','tile'}, dimensions={0} | all-to-all | bytes 393216 | tf_op jit(solution)/shard_map/all_to_all | solution.py:241
  17.9 2.8 %image.1 = f32[8,2,2,128]{3,2,1,0:T(2,128)S(1)} custom-call(bf16[8,2,24,256]{3,2,1,0:T(8,128)(2,1)S(1)} %bitcast.4), custom_call_target="tpu_custom_call" | custom-call | tf_op jit(solution)/shard_map/image/pallas_call | solution.py:243
  20.7 9.1 %all_to_all.11.parts_ref = f32[16,2,128]{2,1,0:T(2,128)S(1)} all-to-all(f32[16,2,128]{2,1,0:T(2,128)S(1)} %bitcast.6), channel_id=1, replica_groups=mesh['group'=2,'src'=8,'tile'=2] {'src','tile'}, dimensions={0} | all-to-all | bytes 32768 | tf_op jit(solution)/shard_map/all_to_all | solution.py:259
  29.8 0.7 %merge_columns.1 = f32[1,8,512]{2,1,0:T(8,128)} custom-call(f32[16,2,128]{2,1,0:T(2,128)S(1)} %all_to_all.11.parts_ref), custom_call_target="tpu_custom_call" | custom-call | tf_op jit(solution)/shard_map/merge_columns/pallas_call | solution.py:260
